TPU v7x, 32 devices: a whole 2x2x4 slice. The times are simulated.
32 devices in a mesh: blk: 8 (over y, x, core), expert: 4 (over z).
Axes of the slice: x: 2, y: 2, z: 4, core: 2. Of those that a mesh axis runs over, the one named last changes fastest.
Arguments:
- queries: bfloat16 [16, 72, 1024], P('expert', None, 'blk'), may hold values from -6 to 6
- keys: bfloat16 [16, 72, 1024], P('expert', None, 'blk'), may hold values from -6 to 6
- values: bfloat16 [16, 72, 1024], P('expert', None, 'blk'), may hold values from -24 to 24
- image_ids: int32 [256], P('blk'), may hold values from 0 to 2, as said below
- placement: int32 [256, 1], P('blk'), may hold values from 0 to 7; in each aligned block of 32 rows (0 to 31, 32 to 63, ...) at most 16 rows name the same one
- merge_gain: float32 [16, 288], P('expert'), may hold values from 0.1 to 1.9
- merge_weight: bfloat16 [16, 288, 2048], P('expert'), may hold values from -0.09375 to 0.09375
- text: bfloat16 [1024, 2048], P('blk'), may hold values from -6 to 6
- norm_gain: float32 [2048], replicated, may hold values from 0.1 to 1.9
- w_gate: bfloat16 [8, 3072, 2048], P('blk', 'expert'), may hold values from -0.125 to 0.125
- w_up: bfloat16 [8, 3072, 2048], P('blk', 'expert'), may hold values from -0.125 to 0.125
- w_down: bfloat16 [8, 3072, 2048], P('blk', 'expert'), may hold values from -0.15625 to 0.15625
- routes: int32 [1024, 8], P('blk'), may hold values from 0 to 127, all different within a row; in each aligned block of 128 rows (0 to 127, 128 to 255, ...) at most 10 rows name the same one
- route_gates: float32 [1024, 8], P('blk'), may hold values from 0.2 to 1
- cotangent: bfloat16 [1024, 2048], P('blk'), may hold values from -6 to 6
Outputs:
- llm_out: bfloat16 [1024, 2048], P('blk')
- attn_grad: float32 [16, 72, 1024], P('expert', None, 'blk')
Inputs may be any that keep to these rules, and one draw needn't show every extreme that they name: `image_ids`: three images in order: ids never fall along the sequence; image 0 holds from 16 to 31 merged rows and image 2 from 17 to 32. `placement`: among the 32 rows of one encoder index no shard is named more than 16 times. `routes`: each token names 8 different experts; among the 128 tokens of one shard no expert is named more than 10 times.
All inputs are finite; a program needn't handle non-finite values.
Results may differ from a plain program's by a relative error of at most 0.03.
Values may be sent and summed in bfloat16 or wider, within the bound.
No kernel may reach another device: no remote copies, remote signals or barrier semaphores. Data moves between devices by JAX's collectives and lax.ppermute only.
A program may use at most 64 MiB of HBM per device.

v0:
```python
import jax
import jax.numpy as jnp
from jax import lax
from jax.sharding import PartitionSpec as P

CAPX = 10


EPS = 1e-06


def block_ranks(hit_table):
    before = jnp.cumsum(hit_table, axis=0) - hit_table
    return jnp.sum(before * hit_table, axis=1)


def body(
    queries,
    keys,
    values,
    image_ids,
    placement,
    merge_gain,
    merge_weight,
    text,
    norm_gain,
    w_gate,
    w_up,
    w_down,
    routes,
    route_gates,
    cotangent,
):
    blocks = lax.axis_size("blk")
    my_index = lax.axis_index("blk")
    expert_size = lax.axis_size("expert")
    expert_index = lax.axis_index("expert")
    heads_here, head_size, patches = queries.shape
    merged_rows = image_ids.shape[0]
    llm_rows, model_width = text.shape
    top_count = routes.shape[1]
    along_width = (((1,), (1,)), ((), ()))
    all_ids, all_dest = (
        lax.all_gather(image_ids, "blk", axis=0, tiled=True),
        lax.all_gather(placement[:, 0], "blk", axis=0, tiled=True),
    )
    patch_ids = jnp.repeat(all_ids, 4)
    my_ids = lax.dynamic_slice_in_dim(patch_ids, my_index * patches, patches, 0)
    score_scale = head_size ** (-0.5)
    run_max = jnp.full((heads_here, patches), -1e30, jnp.float32)
    key_part = lax.all_gather(keys, "blk", axis=2, tiled=True)
    value_part = lax.all_gather(values, "blk", axis=2, tiled=True)
    scores = (
        jnp.einsum("hdq,hdk->hqk", queries, key_part, preferred_element_type=jnp.float32)
        * score_scale
    )
    scores = jnp.where((my_ids[:, None] == patch_ids[None, :])[None], scores, -1e30)
    new_max = jnp.maximum(run_max, jnp.max(scores, axis=-1))
    weights = jnp.exp(scores - new_max[:, :, None])
    run_sum = jnp.sum(weights, axis=-1)
    weighted = jnp.einsum(
        "hqk,hdk->hdq", weights.astype(jnp.bfloat16), value_part, preferred_element_type=jnp.float32
    )
    run_max, run_sum, weighted = (new_max, run_sum, weighted)
    attn = (weighted / run_sum[:, None, :]).astype(jnp.bfloat16)
    spread = jnp.transpose(attn, (2, 0, 1)).reshape(merged_rows, 4, heads_here, head_size)
    merged = (
        jnp.transpose(spread, (0, 2, 1, 3))
        .reshape(merged_rows, heads_here * 4 * head_size)
        .astype(jnp.float32)
    )
    full_width = expert_size * merged.shape[1]
    row_sums, row_squares = lax.psum(
        (jnp.sum(merged, axis=1), jnp.sum(merged * merged, axis=1)), "expert"
    )
    row_mean = row_sums / full_width
    inv_std = lax.rsqrt(row_squares / full_width - row_mean * row_mean + EPS)
    normed = (merged - row_mean[:, None]) * inv_std[:, None]
    gain_flat = merge_gain.reshape(-1)
    scaled = (normed * gain_flat).astype(jnp.bfloat16)
    weight_flat = merge_weight.reshape(-1, merge_weight.shape[2])
    merger_part = jnp.dot(scaled, weight_flat, preferred_element_type=jnp.float32)
    vision = lax.psum(merger_part.astype(jnp.bfloat16), "expert")
    cap_rows = llm_rows // blocks
    long_rows = all_dest.shape[0]
    dest_hits = (all_dest[:, None] == jnp.arange(blocks, dtype=jnp.int32)[None, :]).astype(
        jnp.int32
    )
    slot_index = block_ranks(dest_hits)
    grouped = dest_hits.reshape(blocks, merged_rows, blocks)
    inner_before = jnp.cumsum(grouped, axis=1) - grouped
    block_rank = jnp.sum(inner_before * grouped, axis=2).reshape(long_rows)
    my_dest = lax.dynamic_slice_in_dim(all_dest, my_index * merged_rows, merged_rows, 0)
    local_rank = lax.dynamic_slice_in_dim(block_rank, my_index * merged_rows, merged_rows, 0)
    send_rows = (
        jnp.zeros((blocks, cap_rows, model_width), jnp.bfloat16).at[my_dest, local_rank].set(vision)
    )
    arrived = lax.all_to_all(send_rows, "blk", split_axis=0, concat_axis=0, tiled=True)
    source_block = jnp.arange(long_rows, dtype=jnp.int32) // merged_rows
    arrival = source_block * cap_rows + block_rank
    slot_target = jnp.where(all_dest == my_index, slot_index, llm_rows)
    slot_source = jnp.zeros((llm_rows,), jnp.int32).at[slot_target].set(arrival, mode="drop")
    slot_vision = jnp.zeros((llm_rows,), jnp.bool_).at[slot_target].set(True, mode="drop")
    flat_arrived = arrived.reshape(blocks * cap_rows, model_width)
    hidden_in = jnp.where(slot_vision[:, None], flat_arrived[slot_source], text)
    inputs_f32 = hidden_in.astype(jnp.float32)

    def rms_norm(inputs):
        return (
            inputs * lax.rsqrt(jnp.mean(inputs * inputs, axis=-1, keepdims=True) + EPS) * norm_gain
        )

    normed_h, norm_pull = jax.vjp(rms_norm, inputs_f32)
    h_rows = normed_h.astype(jnp.bfloat16)
    group_count = expert_size // 2
    member = expert_index // group_count
    window = 2 * blocks
    pair_expert = routes.reshape(-1)
    pair_hits = (pair_expert[:, None] == jnp.arange(window, dtype=jnp.int32)[None, :]).astype(
        jnp.int32
    )
    pair_rank = block_ranks(pair_hits)
    pair_live = (pair_expert < window) & (pair_expert % 2 == member)
    slot_count = blocks * CAPX
    pair_slot = jnp.where(pair_live, pair_expert // 2 * CAPX + pair_rank, slot_count)
    pair_token = jnp.arange(llm_rows * top_count, dtype=jnp.int32) // top_count
    pair_gate = jnp.where(pair_live, route_gates.reshape(-1), 0.0)
    slot_token = jnp.zeros((slot_count,), jnp.int32).at[pair_slot].set(pair_token, mode="drop")
    slot_gate = jnp.zeros((slot_count,), jnp.float32).at[pair_slot].set(pair_gate, mode="drop")
    slot_live = jnp.zeros((slot_count,), jnp.float32).at[pair_slot].set(1.0, mode="drop")

    def dispatch(slot_rows):
        buffer = jnp.where(slot_live[:, None] > 0.0, slot_rows, jnp.zeros_like(slot_rows))
        landed = lax.all_to_all(
            buffer.reshape(blocks, CAPX, model_width),
            "blk",
            split_axis=0,
            concat_axis=0,
            tiled=True,
        )
        return landed.reshape(slot_count, model_width)

    def combine(landed, slot_weight):
        weighted_rows = (
            landed.reshape(slot_count, model_width).astype(jnp.float32) * slot_weight[:, None]
        )
        return jnp.zeros((llm_rows, model_width), jnp.float32).at[slot_token].add(weighted_rows)

    def to_owner(partial_value, slot_weight):
        returned = lax.all_to_all(
            partial_value.astype(jnp.bfloat16).reshape(blocks, CAPX, model_width),
            "blk",
            split_axis=0,
            concat_axis=0,
            tiled=True,
        )
        combined = combine(returned, slot_weight)
        return lax.psum(combined.astype(jnp.bfloat16), "expert").astype(jnp.float32)

    gate_rows = w_gate[0]
    up_rows = w_up[0]
    down_rows = w_down[0]
    expert_rows = dispatch(h_rows[slot_token])
    gate_pre = lax.dot_general(
        expert_rows, gate_rows, along_width, preferred_element_type=jnp.float32
    )
    up_proj = lax.dot_general(expert_rows, up_rows, along_width, preferred_element_type=jnp.float32)
    activated = (jax.nn.silu(gate_pre) * up_proj).astype(jnp.bfloat16)
    down_part = jnp.dot(activated, down_rows, preferred_element_type=jnp.float32)
    expert_sum = to_owner(down_part, slot_gate)
    llm_out = (inputs_f32 + expert_sum).astype(jnp.bfloat16)
    cot_rows = cotangent.astype(jnp.float32)
    back_rows = dispatch((cot_rows[slot_token] * slot_gate[:, None]).astype(jnp.bfloat16))
    act_grad = lax.dot_general(
        back_rows, down_rows, along_width, preferred_element_type=jnp.float32
    )
    sigmoid_gate = jax.nn.sigmoid(gate_pre)
    gate_grad = (
        act_grad * up_proj * sigmoid_gate * (1.0 + gate_pre * (1.0 - sigmoid_gate))
    ).astype(jnp.bfloat16)
    up_grad = (act_grad * gate_pre * sigmoid_gate).astype(jnp.bfloat16)
    row_grad = jnp.dot(gate_grad, gate_rows, preferred_element_type=jnp.float32) + jnp.dot(
        up_grad, up_rows, preferred_element_type=jnp.float32
    )
    hidden_grad = to_owner(row_grad, slot_live)
    input_grad = (cot_rows + norm_pull(hidden_grad)[0]).astype(jnp.bfloat16)
    back_target = jnp.where(slot_vision, slot_source, blocks * cap_rows)
    grad_buffer = (
        jnp.zeros((blocks * cap_rows, model_width), jnp.bfloat16)
        .at[back_target]
        .set(input_grad, mode="drop")
    )
    returned_rows = lax.all_to_all(
        grad_buffer.reshape(blocks, cap_rows, model_width),
        "blk",
        split_axis=0,
        concat_axis=0,
        tiled=True,
    )
    vision_grad = returned_rows[my_dest, local_rank]
    scaled_grad = lax.dot_general(
        vision_grad, weight_flat, along_width, preferred_element_type=jnp.float32
    )
    normed_grad = scaled_grad * gain_flat
    grad_sum, cross_sum = lax.psum(
        (jnp.sum(normed_grad, axis=1), jnp.sum(normed_grad * normed, axis=1)), "expert"
    )
    merged_grad = inv_std[:, None] * (
        normed_grad - (grad_sum / full_width)[:, None] - normed * (cross_sum / full_width)[:, None]
    )
    unfolded = (
        merged_grad.reshape(merged_rows, heads_here, 4, head_size)
        .transpose(0, 2, 1, 3)
        .reshape(patches, heads_here, head_size)
    )
    attn_grad = jnp.transpose(unfolded, (1, 2, 0))
    return (llm_out, attn_grad)


def solution(mesh):
    return jax.shard_map(
        body,
        mesh=mesh,
        in_specs=(
            P("expert", None, "blk"),
            P("expert", None, "blk"),
            P("expert", None, "blk"),
            P("blk"),
            P("blk", None),
            P("expert", None),
            P("expert", None, None),
            P("blk", None),
            P(),
            P("blk", "expert", None),
            P("blk", "expert", None),
            P("blk", "expert", None),
            P("blk", None),
            P("blk", None),
            P("blk", None),
        ),
        out_specs=(P("blk", None), P("expert", None, "blk")),
        check_vma=False,
    )
```

profile of v0, /device:TPU:0, one launch (start us, length us, event | category | flops | bytes accessed | tf_op | source)
XLA Modules:
  0.0 305.2 jit_solution(2919637029804932714)
XLA Ops:
  10.9 10.0 %all-reduce.2 = (s32[256]{0:T(256)}, s32[256]{0:T(256)S(1)}) all-reduce(s32[256]{0:T(256)S(1)} %bitcast_dynamic-update-slice_fusion, s32[256]{0:T(256)S(1)} %dynamic-update-slice.1), channel_id=2, replica_groups=mesh['blk'=8,'expert'=4] {'blk'}, use_global_device_ids=true, to_apply=%add | all-reduce | flops 512 | bytes 4096 | tf_op jit(solution)/shard_map/all_gather | solution.py:45
  21.4 9.5 %all_gather.14 = bf16[4,72,1024]{2,1,0:T(8,128)(2,1)S(1)} all-gather(bf16[4,72,128]{2,1,0:T(8,128)(2,1)} %param.16), channel_id=1, replica_groups=mesh['blk'=8,'expert'=4] {'blk'}, dimensions={2}, use_global_device_ids=true | all-gather | bytes 663552 | tf_op jit(solution)/shard_map/all_gather | solution.py:51
  32.4 9.8 %all_gather.15 = bf16[4,72,1024]{2,1,0:T(8,128)(2,1)S(1)} all-gather(bf16[4,72,128]{2,1,0:T(8,128)(2,1)S(1)} %copy-done.7), channel_id=1, replica_groups=mesh['blk'=8,'expert'=4] {'blk'}, dimensions={2}, use_global_device_ids=true | all-gather | bytes 663552 | tf_op jit(solution)/shard_map/all_gather | solution.py:52
  46.2 12.0 %all-reduce.4 = (f32[32]{0:T(128)S(1)}, f32[32]{0:T(128)S(1)}) all-reduce(f32[32]{0:T(128)S(1)} %multiply_reduce_fusion, f32[32]{0:T(128)S(1)} %reduce_sum.108), channel_id=1, replica_groups=mesh['blk'=8,'expert'=4] {'expert'}, use_global_device_ids=true, to_apply=%region_12.13 | all-reduce | flops 64 | bytes 512 | tf_op jit(solution)/shard_map/psum | solution.py:73
  59.8 4.0 %convolution_convert_fusion = bf16[32,2048]{1,0:T(8,128)(2,1)} fusion(bf16[32,1152]{1,0:T(8,128)(2,1)} %convert_element_type.120, bf16[1152,2048]{1,0:T(8,128)(2,1)} %bitcast.111), kind=kOutput, calls=%fused_computation.29 | convolution fusion | flops 151060480 | bytes 4923392 | tf_op jit(solution)/shard_map/dot_general | solution.py:82
  71.7 4.5 %reduce-window.16 = s32[16,8,128]{2,1,0:T(8,128)S(1)} reduce-window(s32[16,8,128]{2,1,0:T(8,128)S(1)} %fusion.64, s32[]{:T(128)} %constant.125.clone.1), window={size=1x1x128 pad=0_0x0_0x127_0}, to_apply=%region_16.17 | reduce-window | flops 2080768 | bytes 131076 | tf_op jit(solution)/shard_map/reduce-window.2
  80.6 4.5 %scatter_custom_fusion.3 = s32[80]{0:T(128)S(1)} fusion(s32[1024]{0:T(1024)S(1)} %bitcast.122, s32[1024]{0:T(1024)} %add_select_fusion.1, s32[]{:T(128)} %constant.125.clone.1), kind=kCustom, calls=%fused_computation.163 | custom fusion | bytes 832 | tf_op jit(solution)/shard_map/scatter | solution.py:128
  86.6 4.3 %scatter_custom_fusion.4 = f32[80]{0:T(128)S(1)} fusion(s32[1024]{0:T(1024)S(1)} %bitcast.123, f32[1024]{0:T(1024)S(1)} %broadcast.345, f32[]{:T(128)} %constant.137.clone.1), kind=kCustom, calls=%fused_computation.161 | custom fusion | bytes 324 | tf_op jit(solution)/shard_map/scatter | solution.py:130
  91.1 4.3 %scatter_custom_fusion.5 = f32[80]{0:T(128)S(1)} fusion(s32[1024]{0:T(1024)S(1)} %bitcast.124, f32[1024]{0:T(1024)S(1)} %fusion.74, f32[]{:T(128)} %constant.137.clone.1), kind=kCustom, calls=%fused_computation.158 | custom fusion | bytes 324 | tf_op jit(solution)/shard_map/scatter | solution.py:129
  97.7 3.2 %gather_fusion.2 = f32[80,2048]{1,0:T(8,128)} fusion(f32[128,2048]{1,0:T(8,128)} %convert_element_type.133, s32[1024]{0:T(1024)S(1)} %pad_clamp_fusion), kind=kCustom, calls=%fused_computation.2 | custom fusion | bytes 1311040 | tf_op jit(solution)/shard_map/gather | solution.py:173
  104.0 6.3 %scatter_fusion = bf16[8,16,2048]{2,1,0:T(8,128)(2,1)} fusion(bf16[8,16,2048]{2,1,0:T(8,128)(2,1)} %broadcast_in_dim.123, s32[32]{0:T(128)S(1)} %get-tuple-element.23, bf16[32,2048]{1,0:T(8,128)(2,1)} %all-reduce.9.cloned.1.call-done), kind=kCustom, calls=%fused_computation.5 | custom fusion | bytes 393472 | tf_op jit(solution)/shard_map/scatter | solution.py:96
  110.3 4.3 %all-to-all-start = ((bf16[8,16,2048]{2,1,0:T(8,128)(2,1)}), bf16[8,16,2048]{2,1,0:T(8,128)(2,1)}, u32[]{:S(2)}, u32[]{:S(2)}) async-start(bf16[8,16,2048]{2,1,0:T(8,128)(2,1)} %scatter_fusion), calls=%async_computation | async-start | bytes 1048576 | tf_op jit(solution)/shard_map/all_to_all | solution.py:98
  117.8 6.4 %all-to-all-done = bf16[8,16,2048]{2,1,0:T(8,128)(2,1)} async-done(((bf16[8,16,2048]{2,1,0:T(8,128)(2,1)}), bf16[8,16,2048]{2,1,0:T(8,128)(2,1)}, u32[]{:S(2)}, u32[]{:S(2)}) %all-to-all-start) | async-done | bytes 524320 | tf_op jit(solution)/shard_map/all_to_all | solution.py:98
  124.2 3.4 %gather_fusion = bf16[128,2048]{1,0:T(8,128)(2,1)} fusion(bf16[128,2048]{1,0:T(8,128)(2,1)} %bitcast.13, s32[1024]{0:T(1024)S(1)} %pad_clamp_fusion.1), kind=kCustom, calls=%fused_computation | custom fusion | bytes 1049088 | tf_op jit(solution)/shard_map/gather | solution.py:105
  130.9 2.9 gather_fusion.1
  138.0 12.8 %all_to_all.30 = bf16[8,10,2048]{2,1,0:T(8,128)(2,1)} all-to-all(bf16[8,10,2048]{2,1,0:T(8,128)(2,1)S(1)} %get-tuple-element.25), channel_id=1, replica_groups=mesh['blk'=8,'expert'=4] {'blk'}, dimensions={0} | all-to-all | bytes 655360 | tf_op jit(solution)/shard_map/all_to_all | solution.py:134
  150.8 4.1 %all-to-all-start.3 = ((bf16[8,10,2048]{2,1,0:T(8,128)(2,1)}), bf16[8,10,2048]{2,1,0:T(8,128)(2,1)}, u32[]{:S(2)}, u32[]{:S(2)}) async-start(bf16[8,10,2048]{2,1,0:T(8,128)(2,1)} %get-tuple-element.24), calls=%async_computation.3 | async-start | bytes 1048576 | tf_op jit(solution)/shard_map/all_to_all | solution.py:134
  156.9 3.8 %fusion.10 = f32[80,768]{1,0:T(8,128)} fusion(bf16[80,2048]{1,0:T(8,128)(2,1)} %reshape.331, bf16[1,768,2048]{2,1,0:T(8,128)(2,1)} %param.24), kind=kOutput, calls=%fused_computation.23 | convolution fusion | flops 251658240 | bytes 3719168 | tf_op jit(solution)/shard_map/dot_general | solution.py:164
  166.6 3.2 %fusion = f32[80,768]{1,0:T(8,128)S(1)} fusion(bf16[80,2048]{1,0:T(8,128)(2,1)} %reshape.334, bf16[1,768,2048]{2,1,0:T(8,128)(2,1)} %param.26), kind=kOutput, calls=%fused_computation.13 | convolution fusion | flops 251658240 | bytes 3719168 | tf_op jit(solution)/shard_map/dot_general | solution.py:174
  173.8 4.1 %all-to-all-start.4 = ((bf16[8,10,2048]{2,1,0:T(8,128)(2,1)}), bf16[8,10,2048]{2,1,0:T(8,128)(2,1)}, u32[]{:S(2)}, u32[]{:S(2)}) async-start(bf16[8,10,2048]{2,1,0:T(8,128)(2,1)} %reshape.335), calls=%async_computation.4 | async-start | bytes 1048576 | tf_op jit(solution)/shard_map/all_to_all | solution.py:150
  178.0 3.5 %fusion.15 = bf16[80,2048]{1,0:T(8,128)(2,1)} fusion(bf16[1,768,2048]{2,1,0:T(8,128)(2,1)} %param.26, f32[80,768]{1,0:T(8,128)} %fusion.6, f32[80,768]{1,0:T(8,128)} %fusion.10), kind=kOutput, calls=%fused_computation.26 | convolution fusion | flops 252190720 | bytes 3964928 | tf_op jit(solution)/shard_map/dot_general | solution.py:169
  183.4 4.3 %all-to-all-done.4 = bf16[8,10,2048]{2,1,0:T(8,128)(2,1)} async-done(((bf16[8,10,2048]{2,1,0:T(8,128)(2,1)}), bf16[8,10,2048]{2,1,0:T(8,128)(2,1)}, u32[]{:S(2)}, u32[]{:S(2)}) %all-to-all-start.4) | async-done | bytes 327712 | tf_op jit(solution)/shard_map/all_to_all | solution.py:150
  187.7 4.1 %all-to-all-start.2 = ((bf16[8,10,2048]{2,1,0:T(8,128)(2,1)}), bf16[8,10,2048]{2,1,0:T(8,128)(2,1)}, u32[]{:S(2)}, u32[]{:S(2)}) async-start(bf16[8,10,2048]{2,1,0:T(8,128)(2,1)} %reshape.332), calls=%async_computation.2 | async-start | bytes 1048576 | tf_op jit(solution)/shard_map/all_to_all | solution.py:150
  193.9 3.2 %scatter_custom_fusion.7 = f32[128,2048]{1,0:T(8,128)} fusion(s32[80]{0:T(128)S(1)} %compare_select_fusion.6, f32[80,2048]{1,0:T(8,128)} %reshape.340, f32[]{:T(128)} %constant.137.clone.1, f32[80]{0:T(128)S(1)} %scatter_custom_fusion.4), kind=kCustom, calls=%fused_computation.59 | custom fusion | flops 327680 | bytes 1704452 | tf_op jit(solution)/shard_map/scatter-add | solution.py:147
  203.6 3.2 %scatter_custom_fusion.6 = f32[128,2048]{1,0:T(8,128)} fusion(s32[80]{0:T(128)S(1)} %compare_select_fusion.6, f32[80,2048]{1,0:T(8,128)} %reshape.339, f32[]{:T(128)} %constant.137.clone.1, f32[80]{0:T(128)S(1)} %scatter_custom_fusion.5), kind=kCustom, calls=%fused_computation.61 | custom fusion | flops 327680 | bytes 1704452 | tf_op jit(solution)/shard_map/scatter-add | solution.py:147
  209.0 48.7 %all-reduce.11.cloned.1.call-done = (bf16[128,2048]{1,0:T(8,128)(2,1)}, bf16[128,2048]{1,0:T(8,128)(2,1)}) async-done(((bf16[128,2048]{1,0:T(8,128)(2,1)}, bf16[128,2048]{1,0:T(8,128)(2,1)}), (bf16[128,2048]{1,0:T(8,128)(2,1)}, bf16[128,2048]{1,0:T(8,128)(2,1)})) %all-reduce.11.cloned.1.call-update) | async-done | bytes 1048592 | tf_op jit(solution)/shard_map/psum | solution.py:158
  257.6 2.4 fusion.34
  260.1 3.3 %scatter_custom_fusion.8 = bf16[128,2048]{1,0:T(8,128)(2,1)} fusion(s32[128]{0:T(128)S(1)} %get-tuple-element.26, bf16[128,2048]{1,0:T(8,128)(2,1)} %copy-done.2, bf16[128,2048]{1,0:T(8,128)(2,1)} %get-tuple-element.17, f32[128]{0:T(128)S(1)} %multiply_multiply_fusion, f32[2048]{0:T(1024)S(1)} %copy-done.6, f32[128]{0:T(128)S(1)} %fusion.91, ...), kind=kCustom, calls=%fused_computation.64 | custom fusion | flops 2621440 | bytes 2106370 | tf_op jit(solution)/shard_map/scatter | solution.py:191
  263.3 4.1 %all-to-all-start.5 = ((bf16[8,16,2048]{2,1,0:T(8,128)(2,1)}), bf16[8,16,2048]{2,1,0:T(8,128)(2,1)}, u32[]{:S(2)}, u32[]{:S(2)}) async-start(bf16[8,16,2048]{2,1,0:T(8,128)(2,1)} %bitcast.116), calls=%async_computation.5 | async-start | bytes 1048576 | tf_op jit(solution)/shard_map/all_to_all | solution.py:193
  269.5 7.7 %all-to-all-done.5 = bf16[8,16,2048]{2,1,0:T(8,128)(2,1)} async-done(((bf16[8,16,2048]{2,1,0:T(8,128)(2,1)}), bf16[8,16,2048]{2,1,0:T(8,128)(2,1)}, u32[]{:S(2)}, u32[]{:S(2)}) %all-to-all-start.5) | async-done | bytes 524320 | tf_op jit(solution)/shard_map/all_to_all | solution.py:193
  279.6 4.0 %fusion.98 = (f32[32]{0:T(128)S(1)}, f32[32]{0:T(128)S(1)}, f32[32,1152]{1,0:T(8,128)S(1)}) fusion(f32[32]{0:T(128)S(1)} %copy-done.14, f32[32,1152]{1,0:T(8,128)S(1)} %reshape.341, f32[32]{0:T(128)S(1)} %copy-done.12, f32[1152]{0:T(1024)S(1)} %mul.255, bf16[32,2048]{1,0:T(8,128)(2,1)} %gather_fusion.3, bf16[1152,2048]{1,0:T(8,128)(2,1)} %bitcast.112), kind=kOutput, calls=%fused_computation.177 | convolution fusion | flops 151216064 | bytes 5149696 | tf_op jit(solution)/shard_map/dot_general | solution.py:201
  283.6 10.2 %all-reduce.3 = (f32[32]{0:T(128)S(1)}, f32[32]{0:T(128)S(1)}) all-reduce(f32[32]{0:T(128)S(1)} %get-tuple-element.9, f32[32]{0:T(128)S(1)} %get-tuple-element.8), channel_id=1, replica_groups=mesh['blk'=8,'expert'=4] {'expert'}, use_global_device_ids=true, to_apply=%region_32.33 | all-reduce | flops 64 | bytes 512 | tf_op jit(solution)/shard_map/psum | solution.py:205
  (132 shorter events, 73.9 us)
Async XLA Ops:
  7.2 153.5 %copy-start = (bf16[1,768,2048]{2,1,0:T(8,128)(2,1)S(1)}, bf16[1,768,2048]{2,1,0:T(8,128)(2,1)}, u32[]{:S(2)}) copy-start(bf16[1,768,2048]{2,1,0:T(8,128)(2,1)} %param.25) | copy-start | bytes 9437188
  7.2 25.3 %copy-start.7 = (bf16[4,72,128]{2,1,0:T(8,128)(2,1)S(1)}, bf16[4,72,128]{2,1,0:T(8,128)(2,1)}, u32[]{:S(2)}) copy-start(bf16[4,72,128]{2,1,0:T(8,128)(2,1)} %param.17) | copy-start | bytes 221188
  7.2 96.0 %all-reduce.9.cloned.1.call-start = ((), (), s32[]{:S(2)}) async-start(), calls=%async_computation.6 | async-start | bytes 262144 | tf_op jit(solution)/shard_map/psum | solution.py:83
  44.2 19.5 %copy-start.15 = (s32[128,8]{0,1:T(8,128)S(1)}, s32[128,8]{0,1:T(8,128)}, u32[]{:S(2)}) copy-start(s32[128,8]{0,1:T(8,128)} %param.27) | copy-start | bytes 12292
  44.5 22.0 %copy-start.9 = (s32[256]{0:T(256)S(1)}, s32[256]{0:T(256)}, u32[]{:S(2)}) copy-start(s32[256]{0:T(256)} %get-tuple-element.10) | copy-start | bytes 3076
  58.2 0.5 copy-start.11
  58.2 0.5 copy-start.13
  97.6 5.4 %copy-start.10 = (s32[256]{0:T(256)S(1)}, s32[256]{0:T(256)}, u32[]{:S(2)}) copy-start(s32[256]{0:T(256)} %get-tuple-element.10) | copy-start | bytes 3076
  110.3 13.9 %all-to-all-start = ((bf16[8,16,2048]{2,1,0:T(8,128)(2,1)}), bf16[8,16,2048]{2,1,0:T(8,128)(2,1)}, u32[]{:S(2)}, u32[]{:S(2)}) async-start(bf16[8,16,2048]{2,1,0:T(8,128)(2,1)} %scatter_fusion), calls=%async_computation | async-start | bytes 1048576 | tf_op jit(solution)/shard_map/all_to_all | solution.py:98
  124.2 5.7 %copy-start.6 = (f32[2048]{0:T(1024)S(1)}, f32[2048]{0:T(1024)}, u32[]{:S(2)}) copy-start(f32[2048]{0:T(1024)} %param.23) | copy-start | bytes 24580
  129.1 0.8 copy-start.2
  150.8 13.9 %all-to-all-start.3 = ((bf16[8,10,2048]{2,1,0:T(8,128)(2,1)}), bf16[8,10,2048]{2,1,0:T(8,128)(2,1)}, u32[]{:S(2)}, u32[]{:S(2)}) async-start(bf16[8,10,2048]{2,1,0:T(8,128)(2,1)} %get-tuple-element.24), calls=%async_computation.3 | async-start | bytes 1048576 | tf_op jit(solution)/shard_map/all_to_all | solution.py:134
  156.9 3.8 %copy-start.4 = (bf16[80,2048]{1,0:T(8,128)(2,1)S(1)}, bf16[80,2048]{1,0:T(8,128)(2,1)}, u32[]{:S(2)}) copy-start(bf16[80,2048]{1,0:T(8,128)(2,1)} %reshape.331) | copy-start | bytes 983044
  166.6 3.2 %copy-start.3 = (f32[80,768]{1,0:T(8,128)S(1)}, f32[80,768]{1,0:T(8,128)}, u32[]{:S(2)}) copy-start(f32[80,768]{1,0:T(8,128)} %fusion.10) | copy-start | bytes 737284
  166.6 3.9 %copy-start.1 = (bf16[1,768,2048]{2,1,0:T(8,128)(2,1)S(1)}, bf16[1,768,2048]{2,1,0:T(8,128)(2,1)}, u32[]{:S(2)}) copy-start(bf16[1,768,2048]{2,1,0:T(8,128)(2,1)} %param.24) | copy-start | bytes 9437188
  166.6 3.9 %copy-start.5 = (f32[80,768]{1,0:T(8,128)S(1)}, f32[80,768]{1,0:T(8,128)}, u32[]{:S(2)}) copy-start(f32[80,768]{1,0:T(8,128)} %fusion.6) | copy-start | bytes 737284
  173.8 13.9 %all-to-all-start.4 = ((bf16[8,10,2048]{2,1,0:T(8,128)(2,1)}), bf16[8,10,2048]{2,1,0:T(8,128)(2,1)}, u32[]{:S(2)}, u32[]{:S(2)}) async-start(bf16[8,10,2048]{2,1,0:T(8,128)(2,1)} %reshape.335), calls=%async_computation.4 | async-start | bytes 1048576 | tf_op jit(solution)/shard_map/all_to_all | solution.py:150
  187.7 13.9 %all-to-all-start.2 = ((bf16[8,10,2048]{2,1,0:T(8,128)(2,1)}), bf16[8,10,2048]{2,1,0:T(8,128)(2,1)}, u32[]{:S(2)}, u32[]{:S(2)}) async-start(bf16[8,10,2048]{2,1,0:T(8,128)(2,1)} %reshape.332), calls=%async_computation.2 | async-start | bytes 1048576 | tf_op jit(solution)/shard_map/all_to_all | solution.py:150
  191.9 65.8 %all-reduce.11.cloned.1.call-start = ((), (), s32[]{:S(2)}) async-start(), calls=%async_computation.7 | async-start | bytes 2097152 | tf_op jit(solution)/shard_map/psum | solution.py:158
  209.0 58.5 %copy-start.8 = (f32[4,288]{1,0:T(4,128)S(1)}, f32[4,288]{1,0:T(4,128)}, u32[]{:S(2)}) copy-start(f32[4,288]{1,0:T(4,128)} %param.20) | copy-start | bytes 13828
  260.1 19.5 %copy-start.12 = (f32[32]{0:T(128)S(1)}, f32[32]{0:T(128)}, u32[]{:S(2)}) copy-start(f32[32]{0:T(128)} %copy-done.11) | copy-start | bytes 388
  260.1 19.5 %copy-start.14 = (f32[32]{0:T(128)S(1)}, f32[32]{0:T(128)}, u32[]{:S(2)}) copy-start(f32[32]{0:T(128)} %copy-done.13) | copy-start | bytes 388
  263.3 13.9 %all-to-all-start.5 = ((bf16[8,16,2048]{2,1,0:T(8,128)(2,1)}), bf16[8,16,2048]{2,1,0:T(8,128)(2,1)}, u32[]{:S(2)}, u32[]{:S(2)}) async-start(bf16[8,16,2048]{2,1,0:T(8,128)(2,1)} %bitcast.116), calls=%async_computation.5 | async-start | bytes 1048576 | tf_op jit(solution)/shard_map/all_to_all | solution.py:193
Sparse Core Ops, SparseCore 0:
  63.9 31.7 all-reduce.8
  209.1 48.5 all-reduce.10
where the time goes:
time: 307 us; the launch traced here: 305 us
  waiting for transfers between devices  71.8 us (23%)
  local copies, waits for them, and re-layouts  68.9 us (22%)
  blocking collectives  64.3 us (21%)
  other arithmetic  39 us (13%)
  matrix products  25.2 us (8%)
  starting transfers between devices  21 us (7%)
  between operations  15.1 us (5%)
    psum x1, waiting for transfers between devices, to_owner(): return lax.psum(combined.astype(jnp.bfloat16), 'expert').astype(jnp.float32)  48.7 us
    all_to_all x1, blocking collectives, dispatch(): lax.all_to_all(buffer.reshape(blocks, CAPX, model_width), 'blk', split_ax...  12.8 us
    psum x1, blocking collectives, body(): lax.psum((jnp.sum(merged, axis=1), jnp.sum(merged * merged, axis=1)), 'ex...  12 us
    psum x1, blocking collectives, body(): lax.psum((jnp.sum(normed_grad, axis=1), jnp.sum(normed_grad * normed, axi...  10.2 us
    all_gather x1, blocking collectives, body(): lax.all_gather(placement[:, 0], 'blk', axis=0, tiled=True)  10 us
    all_gather x1, blocking collectives, body(): value_part = lax.all_gather(values, 'blk', axis=2, tiled=True)  9.8 us
    all_gather x1, blocking collectives, body(): key_part = lax.all_gather(keys, 'blk', axis=2, tiled=True)  9.5 us
    all_to_all x2, starting transfers between devices, to_owner(): lax.all_to_all(partial_value.astype(jnp.bfloat16).reshape(blocks, CAPX, m...  8.28 us
  transfers between devices with their start and end apart: 7, of which 6 were waited for; matrix products, arithmetic and copies ran while one was open for 21% of the time, Pallas kernels for 0%

commit v1 on v0

--- a/solution.py
+++ b/solution.py
@@ -12,6 +12,41 @@
 def block_ranks(hit_table):
     before = jnp.cumsum(hit_table, axis=0) - hit_table
     return jnp.sum(before * hit_table, axis=1)
+
+
+def swap(value, axis, step):
+    count = lax.axis_size(axis)
+    return lax.ppermute(value, axis, [(i, i ^ step) for i in range(count)])
+
+
+def gather_near(value, axis):
+    count = lax.axis_size(axis)
+    return [value] + [swap(value, axis, step) for step in range(1, count)]
+
+
+def exchange(blocks, axis):
+    count = lax.axis_size(axis)
+    parts = [blocks[0]] + [swap(blocks[step], axis, step) for step in range(1, count)]
+    return jnp.stack(parts)
+
+
+def in_order(stacked, axis):
+    count = lax.axis_size(axis)
+    return stacked[jnp.arange(count, dtype=jnp.int32) ^ lax.axis_index(axis)]
+
+
+def small_sum(value, axis):
+    parts = gather_near(value, axis)
+    return sum(parts[1:], parts[0])
+
+
+def wide_sum(value, axis):
+    count = lax.axis_size(axis)
+    rows, width = value.shape
+    pieces = in_order(value.reshape(count, rows // count, width), axis)
+    mine = exchange(pieces, axis).astype(jnp.float32).sum(axis=0).astype(value.dtype)
+    whole = jnp.stack(gather_near(mine, axis))
+    return in_order(whole, axis).reshape(rows, width)
 
 
 def body(
@@ -40,21 +75,19 @@
     llm_rows, model_width = text.shape
     top_count = routes.shape[1]
     along_width = (((1,), (1,)), ((), ()))
-    all_ids, all_dest = (
-        lax.all_gather(image_ids, "blk", axis=0, tiled=True),
-        lax.all_gather(placement[:, 0], "blk", axis=0, tiled=True),
-    )
-    patch_ids = jnp.repeat(all_ids, 4)
-    my_ids = lax.dynamic_slice_in_dim(patch_ids, my_index * patches, patches, 0)
+    marks = jnp.stack(gather_near(jnp.stack([image_ids, placement[:, 0]]), "blk"))
+    near_ids = jnp.repeat(marks[:, 0].reshape(-1), 4)
+    all_dest = in_order(marks[:, 1], "blk").reshape(-1)
+    my_ids = near_ids[:patches]
     score_scale = head_size ** (-0.5)
     run_max = jnp.full((heads_here, patches), -1e30, jnp.float32)
-    key_part = lax.all_gather(keys, "blk", axis=2, tiled=True)
-    value_part = lax.all_gather(values, "blk", axis=2, tiled=True)
+    key_part = jnp.concatenate(gather_near(keys, "blk"), axis=2)
+    value_part = jnp.concatenate(gather_near(values, "blk"), axis=2)
     scores = (
         jnp.einsum("hdq,hdk->hqk", queries, key_part, preferred_element_type=jnp.float32)
         * score_scale
     )
-    scores = jnp.where((my_ids[:, None] == patch_ids[None, :])[None], scores, -1e30)
+    scores = jnp.where((my_ids[:, None] == near_ids[None, :])[None], scores, -1e30)
     new_max = jnp.maximum(run_max, jnp.max(scores, axis=-1))
     weights = jnp.exp(scores - new_max[:, :, None])
     run_sum = jnp.sum(weights, axis=-1)
@@ -70,8 +103,8 @@
         .astype(jnp.float32)
     )
     full_width = expert_size * merged.shape[1]
-    row_sums, row_squares = lax.psum(
-        (jnp.sum(merged, axis=1), jnp.sum(merged * merged, axis=1)), "expert"
+    row_sums, row_squares = small_sum(
+        jnp.stack([jnp.sum(merged, axis=1), jnp.sum(merged * merged, axis=1)]), "expert"
     )
     row_mean = row_sums / full_width
     inv_std = lax.rsqrt(row_squares / full_width - row_mean * row_mean + EPS)
@@ -80,7 +113,7 @@
     scaled = (normed * gain_flat).astype(jnp.bfloat16)
     weight_flat = merge_weight.reshape(-1, merge_weight.shape[2])
     merger_part = jnp.dot(scaled, weight_flat, preferred_element_type=jnp.float32)
-    vision = lax.psum(merger_part.astype(jnp.bfloat16), "expert")
+    vision = wide_sum(merger_part.astype(jnp.bfloat16), "expert")
     cap_rows = llm_rows // blocks
     long_rows = all_dest.shape[0]
     dest_hits = (all_dest[:, None] == jnp.arange(blocks, dtype=jnp.int32)[None, :]).astype(
@@ -93,11 +126,13 @@
     my_dest = lax.dynamic_slice_in_dim(all_dest, my_index * merged_rows, merged_rows, 0)
     local_rank = lax.dynamic_slice_in_dim(block_rank, my_index * merged_rows, merged_rows, 0)
     send_rows = (
-        jnp.zeros((blocks, cap_rows, model_width), jnp.bfloat16).at[my_dest, local_rank].set(vision)
-    )
-    arrived = lax.all_to_all(send_rows, "blk", split_axis=0, concat_axis=0, tiled=True)
+        jnp.zeros((blocks, cap_rows, model_width), jnp.bfloat16)
+        .at[my_dest ^ my_index, local_rank]
+        .set(vision)
+    )
+    arrived = exchange(send_rows, "blk")
     source_block = jnp.arange(long_rows, dtype=jnp.int32) // merged_rows
-    arrival = source_block * cap_rows + block_rank
+    arrival = (source_block ^ my_index) * cap_rows + block_rank
     slot_target = jnp.where(all_dest == my_index, slot_index, llm_rows)
     slot_source = jnp.zeros((llm_rows,), jnp.int32).at[slot_target].set(arrival, mode="drop")
     slot_vision = jnp.zeros((llm_rows,), jnp.bool_).at[slot_target].set(True, mode="drop")
@@ -122,7 +157,7 @@
     pair_rank = block_ranks(pair_hits)
     pair_live = (pair_expert < window) & (pair_expert % 2 == member)
     slot_count = blocks * CAPX
-    pair_slot = jnp.where(pair_live, pair_expert // 2 * CAPX + pair_rank, slot_count)
+    pair_slot = jnp.where(pair_live, (pair_expert // 2 ^ my_index) * CAPX + pair_rank, slot_count)
     pair_token = jnp.arange(llm_rows * top_count, dtype=jnp.int32) // top_count
     pair_gate = jnp.where(pair_live, route_gates.reshape(-1), 0.0)
     slot_token = jnp.zeros((slot_count,), jnp.int32).at[pair_slot].set(pair_token, mode="drop")
@@ -131,13 +166,7 @@
 
     def dispatch(slot_rows):
         buffer = jnp.where(slot_live[:, None] > 0.0, slot_rows, jnp.zeros_like(slot_rows))
-        landed = lax.all_to_all(
-            buffer.reshape(blocks, CAPX, model_width),
-            "blk",
-            split_axis=0,
-            concat_axis=0,
-            tiled=True,
-        )
+        landed = exchange(buffer.reshape(blocks, CAPX, model_width), "blk")
         return landed.reshape(slot_count, model_width)
 
     def combine(landed, slot_weight):
@@ -147,15 +176,11 @@
         return jnp.zeros((llm_rows, model_width), jnp.float32).at[slot_token].add(weighted_rows)
 
     def to_owner(partial_value, slot_weight):
-        returned = lax.all_to_all(
-            partial_value.astype(jnp.bfloat16).reshape(blocks, CAPX, model_width),
-            "blk",
-            split_axis=0,
-            concat_axis=0,
-            tiled=True,
+        returned = exchange(
+            partial_value.astype(jnp.bfloat16).reshape(blocks, CAPX, model_width), "blk"
         )
         combined = combine(returned, slot_weight)
-        return lax.psum(combined.astype(jnp.bfloat16), "expert").astype(jnp.float32)
+        return wide_sum(combined.astype(jnp.bfloat16), "expert").astype(jnp.float32)
 
     gate_rows = w_gate[0]
     up_rows = w_up[0]
@@ -190,20 +215,15 @@
         .at[back_target]
         .set(input_grad, mode="drop")
     )
-    returned_rows = lax.all_to_all(
-        grad_buffer.reshape(blocks, cap_rows, model_width),
-        "blk",
-        split_axis=0,
-        concat_axis=0,
-        tiled=True,
-    )
-    vision_grad = returned_rows[my_dest, local_rank]
+    returned_rows = exchange(grad_buffer.reshape(blocks, cap_rows, model_width), "blk")
+    vision_grad = returned_rows[my_dest ^ my_index, local_rank]
     scaled_grad = lax.dot_general(
         vision_grad, weight_flat, along_width, preferred_element_type=jnp.float32
     )
     normed_grad = scaled_grad * gain_flat
-    grad_sum, cross_sum = lax.psum(
-        (jnp.sum(normed_grad, axis=1), jnp.sum(normed_grad * normed, axis=1)), "expert"
+    grad_sum, cross_sum = small_sum(
+        jnp.stack([jnp.sum(normed_grad, axis=1), jnp.sum(normed_grad * normed, axis=1)]),
+        "expert",
     )
     merged_grad = inv_std[:, None] * (
         normed_grad - (grad_sum / full_width)[:, None] - normed * (cross_sum / full_width)[:, None]

time: 307 us -> 330 us (1.075)
  starting transfers between devices: 21 us -> 101 us
  local copies, waits for them, and re-layouts: 68.9 us -> 134 us
  blocking collectives: 64.3 us -> 0 us
  waiting for transfers between devices: 71.8 us -> 30.9 us
  between operations: 15.1 us -> 1.5 us
  matrix products: 25.2 us -> 18.6 us
    ppermute x0 -> x87, starting transfers between devices: none -> 101 us  [swap(): return lax.ppermute(value, axis, [(i, i ^ step) for i in range(count)])]
    psum x2 -> x0, waiting for transfers between devices: 48.7 us -> none  [the longest x1 48.7 us: to_owner(): return lax.psum(combined.astype(jnp.bfloat16), 'expert').astype(jnp.float32)]
    unnamed x40 -> x148, local copies, waits for them, and re-layouts: 6.98 us -> 53.5 us
    ppermute x0 -> x87, waiting for transfers between devices: none -> 30.9 us  [swap(): return lax.ppermute(value, axis, [(i, i ^ step) for i in range(count)])]
    all_gather x3 -> x0, blocking collectives: 29.3 us -> none  [the longest x1 10 us: body(): lax.all_gather(placement[:, 0], 'blk', axis=0, tiled=True)]
    all_to_all x5 -> x0, waiting for transfers between devices: 23 us -> none  [the longest x1 7.72 us: body(): lax.all_to_all(grad_buffer.reshape(blocks, cap_rows, model_width), 'blk',...]
    psum x2 -> x0, blocking collectives: 22.1 us -> none  [the longest x1 12 us: body(): lax.psum((jnp.sum(merged, axis=1), jnp.sum(merged * merged, axis=1)), 'ex...]
    all_to_all x5 -> x0, starting transfers between devices: 20.9 us -> none  [the longest x2 8.28 us: to_owner(): lax.all_to_all(partial_value.astype(jnp.bfloat16).reshape(blocks, CAPX, m...]
  transfers between devices with their start and end apart: 7 -> 87, of which waited for: 6 -> 13; matrix products, arithmetic and copies ran while one was open for 21% -> 41% of each run, Pallas kernels for 0% -> 0%
where the time goes in v1:
time: 330 us; the launch traced here: 327 us
  local copies, waits for them, and re-layouts  134 us (41%)
  starting transfers between devices  101 us (31%)
  other arithmetic  41.4 us (13%)
  waiting for transfers between devices  30.9 us (9%)
  matrix products  18.6 us (6%)
    ppermute x87, starting transfers between devices, swap(): return lax.ppermute(value, axis, [(i, i ^ step) for i in range(count)])  101 us
    unnamed x148, local copies, waits for them, and re-layouts  53.5 us
    ppermute x87, waiting for transfers between devices, swap(): return lax.ppermute(value, axis, [(i, i ^ step) for i in range(count)])  30.9 us
    gather x8, local copies, waits for them, and re-layouts, in_order(): return stacked[jnp.arange(count, dtype=jnp.int32) ^ lax.axis_index(axis)]  13.7 us
    scatter-add x2, other arithmetic, combine(): jnp.zeros((llm_rows, model_width), jnp.float32).at[slot_token]  6.68 us
  transfers between devices with their start and end apart: 87, of which 13 were waited for; matrix products, arithmetic and copies ran while one was open for 41% of the time, Pallas kernels for 0%

profile of v1, /device:TPU:0, one launch (start us, length us, event | category | flops | bytes accessed | tf_op | source)
XLA Modules:
  0.0 327.1 jit_solution(16412551042039367859)
XLA Ops:
  1.5 3.0 collective-permute-start.3
  14.6 4.5 %reduce-window.16 = s32[16,8,128]{2,1,0:T(8,128)S(1)} reduce-window(s32[16,8,128]{2,1,0:T(8,128)S(1)} %fusion.69, s32[]{:T(128)} %constant.128.clone.1), window={size=1x1x128 pad=0_0x0_0x127_0}, to_apply=%region_13.14 | reduce-window | flops 2080768 | bytes 131076 | tf_op jit(solution)/shard_map/reduce-window.2
  19.6 4.3 %scatter_custom_fusion.3 = s32[80]{0:T(128)S(1)} fusion(s32[1024]{0:T(1024)S(1)} %bitcast.381, s32[1024]{0:T(1024)S(1)} %add_select_fusion.1, s32[]{:T(128)} %constant.128.clone.1), kind=kCustom, calls=%fused_computation.287 | custom fusion | bytes 324 | tf_op jit(solution)/shard_map/scatter | solution.py:163
  24.9 4.8 %scatter_custom_fusion.5 = f32[80]{0:T(128)} fusion(s32[1024]{0:T(1024)S(1)} %bitcast.382, f32[1024]{0:T(1024)S(1)} %fusion.82, f32[]{:T(128)} %constant.139.clone.1), kind=kCustom, calls=%fused_computation.282 | custom fusion | bytes 324 | tf_op jit(solution)/shard_map/scatter | solution.py:164
  29.7 4.3 %scatter_custom_fusion.4 = f32[80]{0:T(128)S(1)} fusion(s32[1024]{0:T(1024)S(1)} %bitcast.383, f32[1024]{0:T(1024)S(1)} %broadcast.462, f32[]{:T(128)} %constant.139.clone.1), kind=kCustom, calls=%fused_computation.285 | custom fusion | bytes 324 | tf_op jit(solution)/shard_map/scatter | solution.py:165
  37.4 3.2 gather_fusion.7
  71.7 2.6 collective-permute-done.12
  74.3 2.5 collective-permute-done.13
  81.0 2.6 collective-permute-start.22
  85.6 3.3 %collective-permute-done.23 = f32[2,32]{1,0:T(2,128)S(1)} collective-permute-done((f32[2,32]{1,0:T(2,128)S(1)}, f32[2,32]{1,0:T(2,128)S(1)}, u32[]{:S(2)}, u32[]{:S(2)}) %collective-permute-start.23) | collective-permute-done | bytes 288 | tf_op jit(solution)/shard_map/ppermute | solution.py:19
  91.8 3.3 %fusion.21 = bf16[4,8,2048]{2,1,0:T(8,128)(2,1)S(1)} fusion(bf16[32,1152]{1,0:T(8,128)(2,1)} %convert_element_type.131, bf16[1152,2048]{1,0:T(8,128)(2,1)} %bitcast.349), kind=kOutput, calls=%fused_computation.37 | convolution fusion | flops 151060480 | bytes 4923392 | tf_op jit(solution)/shard_map/dot_general | solution.py:115
  98.1 3.5 %collective-permute-start.26 = (bf16[8,2048]{1,0:T(8,128)(2,1)S(1)}, bf16[8,2048]{1,0:T(8,128)(2,1)S(1)}, u32[]{:S(2)}, u32[]{:S(2)}) collective-permute-start(bf16[8,2048]{1,0:T(8,128)(2,1)S(1)} %get-tuple-element.65), channel_id=1, source_target_pairs={{0,3},{1,2},{2,1},{3,0},{4,7},{5,6},{6,5},{7,4},{8,11},{9,10},{10,... | collective-permute-start | bytes 98312 | tf_op jit(solution)/shard_map/ppermute | solution.py:19
  104.9 4.0 %collective-permute-start.28 = (bf16[8,2048]{1,0:T(8,128)(2,1)S(1)}, bf16[8,2048]{1,0:T(8,128)(2,1)S(1)}, u32[]{:S(2)}, u32[]{:S(2)}) collective-permute-start(bf16[8,2048]{1,0:T(8,128)(2,1)S(1)} %fusion.72), channel_id=1, source_target_pairs={{0,2},{1,3},{2,0},{3,1},{4,6},{5,7},{6,4},{7,5},{8,10},{9,11},{10,... | collective-permute-start | bytes 98312 | tf_op jit(solution)/shard_map/ppermute | solution.py:19
  111.2 3.5 %collective-permute-done.29 = bf16[8,2048]{1,0:T(8,128)(2,1)S(1)} collective-permute-done((bf16[8,2048]{1,0:T(8,128)(2,1)S(1)}, bf16[8,2048]{1,0:T(8,128)(2,1)S(1)}, u32[]{:S(2)}, u32[]{:S(2)}) %collective-permute-start.29) | collective-permute-done | bytes 32800 | tf_op jit(solution)/shard_map/ppermute | solution.py:19
  118.3 6.3 %scatter_fusion = bf16[8,16,2048]{2,1,0:T(8,128)(2,1)} fusion(bf16[8,16,2048]{2,1,0:T(8,128)(2,1)} %broadcast_in_dim.126, s32[32]{0:T(128)S(1)} %get-tuple-element.69, bf16[32,2048]{1,0:T(8,128)(2,1)} %bitcast.358), kind=kCustom, calls=%fused_computation.12 | custom fusion | bytes 393472 | tf_op jit(solution)/shard_map/scatter | solution.py:131
  140.5 3.5 %gather_fusion.3 = bf16[128,2048]{1,0:T(8,128)(2,1)} fusion(bf16[128,2048]{1,0:T(8,128)(2,1)} %bitcast.348, s32[1024]{0:T(1024)} %pad_clamp_fusion.1), kind=kCustom, calls=%fused_computation.3 | custom fusion | bytes 1049088 | tf_op jit(solution)/shard_map/gather | solution.py:140
  147.3 3.1 gather_fusion.4
  170.4 3.2 fusion.10
  212.9 3.4 %scatter_custom_fusion.6 = f32[128,2048]{1,0:T(8,128)} fusion(s32[80]{0:T(128)} %copy-done.44, f32[80,2048]{1,0:T(8,128)} %reshape.533, f32[]{:T(128)} %constant.139.clone.1, f32[80]{0:T(128)S(1)} %copy-done.33), kind=kCustom, calls=%fused_computation.67 | custom fusion | flops 327680 | bytes 1704768 | tf_op jit(solution)/shard_map/scatter-add | solution.py:176
  231.7 3.5 %collective-permute-start.53 = (bf16[32,2048]{1,0:T(8,128)(2,1)}, bf16[32,2048]{1,0:T(8,128)(2,1)}, u32[]{:S(2)}, u32[]{:S(2)}) collective-permute-start(bf16[32,2048]{1,0:T(8,128)(2,1)} %get-tuple-element.26), channel_id=1, source_target_pairs={{0,3},{1,2},{2,1},{3,0},{4,7},{5,6},{6,5},{7,4},{8,11},{9,10},{10,... | collective-permute-start | bytes 393224 | tf_op jit(solution)/shard_map/ppermute | solution.py:19
  239.9 3.2 scatter_custom_fusion.7
  245.2 2.4 gather_fusion.8
  249.7 3.5 %collective-permute-start.73 = (bf16[32,2048]{1,0:T(8,128)(2,1)S(1)}, bf16[32,2048]{1,0:T(8,128)(2,1)S(1)}, u32[]{:S(2)}, u32[]{:S(2)}) collective-permute-start(bf16[32,2048]{1,0:T(8,128)(2,1)S(1)} %get-tuple-element.23), channel_id=1, source_target_pairs={{0,3},{1,2},{2,1},{3,0},{4,7},{5,6},{6,5},{7,4},{8,11},{9,10},{10,... | collective-permute-start | bytes 393224 | tf_op jit(solution)/shard_map/ppermute | solution.py:19
  255.6 3.1 collective-permute-start.56
  258.7 4.4 %collective-permute-done.72 = bf16[32,2048]{1,0:T(8,128)(2,1)S(1)} collective-permute-done((bf16[32,2048]{1,0:T(8,128)(2,1)S(1)}, bf16[32,2048]{1,0:T(8,128)(2,1)S(1)}, u32[]{:S(2)}, u32[]{:S(2)}) %collective-permute-start.72) | collective-permute-done | bytes 131104 | tf_op jit(solution)/shard_map/ppermute | solution.py:19
  264.1 7.7 %collective-permute-start.74 = (bf16[32,2048]{1,0:T(8,128)(2,1)S(1)}, bf16[32,2048]{1,0:T(8,128)(2,1)}, u32[]{:S(2)}, u32[]{:S(2)}) collective-permute-start(bf16[32,2048]{1,0:T(8,128)(2,1)S(1)} %fusion.57), channel_id=1, source_target_pairs={{0,1},{1,0},{2,3},{3,2},{4,5},{5,4},{6,7},{7,6},{8,9},{9,8},{10,11... | collective-permute-start | bytes 393224 | tf_op jit(solution)/shard_map/ppermute | solution.py:19
  278.5 5.9 %collective-permute-done.75 = bf16[32,2048]{1,0:T(8,128)(2,1)} collective-permute-done((bf16[32,2048]{1,0:T(8,128)(2,1)S(1)}, bf16[32,2048]{1,0:T(8,128)(2,1)}, u32[]{:S(2)}, u32[]{:S(2)}) %collective-permute-start.75) | collective-permute-done | bytes 131104 | tf_op jit(solution)/shard_map/ppermute | solution.py:19
  286.3 2.4 gather_fusion.9
  291.2 3.3 %scatter_custom_fusion.8 = bf16[128,2048]{1,0:T(8,128)(2,1)} fusion(s32[128]{0:T(128)} %get-tuple-element.76, bf16[128,2048]{1,0:T(8,128)(2,1)} %copy-done.4, bf16[128,2048]{1,0:T(8,128)(2,1)} %bitcast.351, f32[128]{0:T(128)S(1)} %multiply_multiply_fusion, f32[2048]{0:T(1024)S(1)} %copy-done.9, f32[128]{0:T(128)S(1)} %copy-done.35, ...), kind=kCustom, calls=%fused_computation.69 | custom fusion | flops 2621440 | bytes 2106880 | tf_op jit(solution)/shard_map/scatter | solution.py:216
  310.6 3.9 %fusion.110 = (f32[32]{0:T(128)S(1)}, f32[32]{0:T(128)S(1)}, f32[32,1152]{1,0:T(8,128)S(1)}) fusion(f32[32]{0:T(128)S(1)} %copy-done.29, f32[32,1152]{1,0:T(8,128)S(1)} %reshape.537, f32[32]{0:T(128)S(1)} %copy-done.31, f32[1152]{0:T(1024)S(1)} %copy-done.21, bf16[32,2048]{1,0:T(8,128)(2,1)S(1)} %gather_fusion.10, bf16[1152,2048]{1,0:T(8,128)(2,1)} %bitcast.350), kind=kOutput, calls=%fused_computation.297 | convolution fusion | flops 151216064 | bytes 5149696 | tf_op jit(solution)/shard_map/dot_general | solution.py:220
  314.6 2.5 collective-permute-start.84
  317.0 2.4 collective-permute-start.86
  (433 shorter events, 208.3 us)
Async XLA Ops:
  1.5 39.1 %collective-permute-start.3 = (s32[2,32]{1,0:T(2,128)S(1)}, s32[2,32]{1,0:T(2,128)S(1)}, u32[]{:S(2)}, u32[]{:S(2)}) collective-permute-start(s32[2,32]{1,0:T(2,128)S(1)} %get-tuple-element.73), channel_id=1, source_target_pairs={{0,16},{4,20},{8,24},{12,28},{16,0},{20,4},{24,8},{28,12},{1,17},{... | collective-permute-start | bytes 776 | tf_op jit(solution)/shard_map/ppermute | solution.py:19
  4.4 37.7 %collective-permute-start.4 = (s32[2,32]{1,0:T(2,128)S(1)}, s32[2,32]{1,0:T(2,128)S(1)}, u32[]{:S(2)}, u32[]{:S(2)}) collective-permute-start(s32[2,32]{1,0:T(2,128)S(1)} %get-tuple-element.73), channel_id=1, source_target_pairs={{0,20},{4,16},{8,28},{12,24},{16,4},{20,0},{24,12},{28,8},{1,21},{... | collective-permute-start | bytes 776 | tf_op jit(solution)/shard_map/ppermute | solution.py:19
  4.4 37.7 %collective-permute-start.5 = (s32[2,32]{1,0:T(2,128)S(1)}, s32[2,32]{1,0:T(2,128)S(1)}, u32[]{:S(2)}, u32[]{:S(2)}) collective-permute-start(s32[2,32]{1,0:T(2,128)S(1)} %get-tuple-element.73), channel_id=1, source_target_pairs={{0,24},{4,28},{8,16},{12,20},{16,8},{20,12},{24,0},{28,4},{1,25},{... | collective-permute-start | bytes 776 | tf_op jit(solution)/shard_map/ppermute | solution.py:19
  6.6 36.2 %collective-permute-start.6 = (s32[2,32]{1,0:T(2,128)S(1)}, s32[2,32]{1,0:T(2,128)S(1)}, u32[]{:S(2)}, u32[]{:S(2)}) collective-permute-start(s32[2,32]{1,0:T(2,128)S(1)} %get-tuple-element.73), channel_id=1, source_target_pairs={{0,28},{4,24},{8,20},{12,16},{16,12},{20,8},{24,4},{28,0},{1,29},{... | collective-permute-start | bytes 776 | tf_op jit(solution)/shard_map/ppermute | solution.py:19
  7.2 37.1 %collective-permute-start = (s32[2,32]{1,0:T(2,128)S(1)}, s32[2,32]{1,0:T(2,128)S(1)}, u32[]{:S(2)}, u32[]{:S(2)}) collective-permute-start(s32[2,32]{1,0:T(2,128)S(1)} %get-tuple-element.73), channel_id=1, source_target_pairs={{0,4},{4,0},{8,12},{12,8},{16,20},{20,16},{24,28},{28,24},{1,5},{5... | collective-permute-start | bytes 776 | tf_op jit(solution)/shard_map/ppermute | solution.py:19
  42.8 12.5 %collective-permute-start.15 = (bf16[4,72,128]{2,1,0:T(8,128)(2,1)S(1)}, bf16[4,72,128]{2,1,0:T(8,128)(2,1)}, u32[]{:S(2)}, u32[]{:S(2)}) collective-permute-start(bf16[4,72,128]{2,1,0:T(8,128)(2,1)S(1)} %copy-done.11), channel_id=1, source_target_pairs={{0,8},{4,12},{8,0},{12,4},{16,24},{20,28},{24,16},{28,20},{1,9},{5... | collective-permute-start | bytes 221192 | tf_op jit(solution)/shard_map/ppermute | solution.py:19
  44.3 12.8 %collective-permute-start.16 = (bf16[4,72,128]{2,1,0:T(8,128)(2,1)S(1)}, bf16[4,72,128]{2,1,0:T(8,128)(2,1)}, u32[]{:S(2)}, u32[]{:S(2)}) collective-permute-start(bf16[4,72,128]{2,1,0:T(8,128)(2,1)S(1)} %copy-done.11), channel_id=1, source_target_pairs={{0,12},{4,8},{8,4},{12,0},{16,28},{20,24},{24,20},{28,16},{1,13},{... | collective-permute-start | bytes 221192 | tf_op jit(solution)/shard_map/ppermute | solution.py:19
  44.3 14.9 %collective-permute-start.17 = (bf16[4,72,128]{2,1,0:T(8,128)(2,1)S(1)}, bf16[4,72,128]{2,1,0:T(8,128)(2,1)}, u32[]{:S(2)}, u32[]{:S(2)}) collective-permute-start(bf16[4,72,128]{2,1,0:T(8,128)(2,1)S(1)} %copy-done.11), channel_id=1, source_target_pairs={{0,16},{4,20},{8,24},{12,28},{16,0},{20,4},{24,8},{28,12},{1,17},{... | collective-permute-start | bytes 221192 | tf_op jit(solution)/shard_map/ppermute | solution.py:19
  45.7 16.5 %collective-permute-start.18 = (bf16[4,72,128]{2,1,0:T(8,128)(2,1)S(1)}, bf16[4,72,128]{2,1,0:T(8,128)(2,1)}, u32[]{:S(2)}, u32[]{:S(2)}) collective-permute-start(bf16[4,72,128]{2,1,0:T(8,128)(2,1)S(1)} %copy-done.11), channel_id=1, source_target_pairs={{0,20},{4,16},{8,28},{12,24},{16,4},{20,0},{24,12},{28,8},{1,21},{... | collective-permute-start | bytes 221192 | tf_op jit(solution)/shard_map/ppermute | solution.py:19
  161.3 15.5 %collective-permute-start.57 = (bf16[10,2048]{1,0:T(8,128)(2,1)}, bf16[10,2048]{1,0:T(8,128)(2,1)}, u32[]{:S(2)}, u32[]{:S(2)}) collective-permute-start(bf16[10,2048]{1,0:T(8,128)(2,1)} %get-tuple-element.48), channel_id=1, source_target_pairs={{0,4},{4,0},{8,12},{12,8},{16,20},{20,16},{24,28},{28,24},{1,5},{5... | collective-permute-start | bytes 122888 | tf_op jit(solution)/shard_map/ppermute | solution.py:19
  162.5 18.0 %collective-permute-start.58 = (bf16[10,2048]{1,0:T(8,128)(2,1)}, bf16[10,2048]{1,0:T(8,128)(2,1)}, u32[]{:S(2)}, u32[]{:S(2)}) collective-permute-start(bf16[10,2048]{1,0:T(8,128)(2,1)} %get-tuple-element.47), channel_id=1, source_target_pairs={{0,8},{4,12},{8,0},{12,4},{16,24},{20,28},{24,16},{28,20},{1,9},{5... | collective-permute-start | bytes 122888 | tf_op jit(solution)/shard_map/ppermute | solution.py:19
  164.6 17.7 %collective-permute-start.59 = (bf16[10,2048]{1,0:T(8,128)(2,1)}, bf16[10,2048]{1,0:T(8,128)(2,1)}, u32[]{:S(2)}, u32[]{:S(2)}) collective-permute-start(bf16[10,2048]{1,0:T(8,128)(2,1)} %get-tuple-element.46), channel_id=1, source_target_pairs={{0,12},{4,8},{8,4},{12,0},{16,28},{20,24},{24,20},{28,16},{1,13},{... | collective-permute-start | bytes 122888 | tf_op jit(solution)/shard_map/ppermute | solution.py:19
  165.2 19.2 %collective-permute-start.60 = (bf16[10,2048]{1,0:T(8,128)(2,1)}, bf16[10,2048]{1,0:T(8,128)(2,1)}, u32[]{:S(2)}, u32[]{:S(2)}) collective-permute-start(bf16[10,2048]{1,0:T(8,128)(2,1)} %get-tuple-element.45), channel_id=1, source_target_pairs={{0,16},{4,20},{8,24},{12,28},{16,0},{20,4},{24,8},{28,12},{1,17},{... | collective-permute-start | bytes 122888 | tf_op jit(solution)/shard_map/ppermute | solution.py:19
  167.9 18.0 %collective-permute-start.61 = (bf16[10,2048]{1,0:T(8,128)(2,1)}, bf16[10,2048]{1,0:T(8,128)(2,1)}, u32[]{:S(2)}, u32[]{:S(2)}) collective-permute-start(bf16[10,2048]{1,0:T(8,128)(2,1)} %get-tuple-element.44), channel_id=1, source_target_pairs={{0,20},{4,16},{8,28},{12,24},{16,4},{20,0},{24,12},{28,8},{1,21},{... | collective-permute-start | bytes 122888 | tf_op jit(solution)/shard_map/ppermute | solution.py:19
  182.2 16.9 %collective-permute-start.44 = (bf16[10,2048]{1,0:T(8,128)(2,1)}, bf16[10,2048]{1,0:T(8,128)(2,1)}, u32[]{:S(2)}, u32[]{:S(2)}) collective-permute-start(bf16[10,2048]{1,0:T(8,128)(2,1)} %get-tuple-element.55), channel_id=1, source_target_pairs={{0,4},{4,0},{8,12},{12,8},{16,20},{20,16},{24,28},{28,24},{1,5},{5... | collective-permute-start | bytes 122888 | tf_op jit(solution)/shard_map/ppermute | solution.py:19
  203.7 19.0 %collective-permute-start.64 = (bf16[10,2048]{1,0:T(8,128)(2,1)}, bf16[10,2048]{1,0:T(8,128)(2,1)}, u32[]{:S(2)}, u32[]{:S(2)}) collective-permute-start(bf16[10,2048]{1,0:T(8,128)(2,1)} %get-tuple-element.41), channel_id=1, source_target_pairs={{0,4},{4,0},{8,12},{12,8},{16,20},{20,16},{24,28},{28,24},{1,5},{5... | collective-permute-start | bytes 122888 | tf_op jit(solution)/shard_map/ppermute | solution.py:19
  204.9 21.3 %collective-permute-start.65 = (bf16[10,2048]{1,0:T(8,128)(2,1)S(1)}, bf16[10,2048]{1,0:T(8,128)(2,1)}, u32[]{:S(2)}, u32[]{:S(2)}) collective-permute-start(bf16[10,2048]{1,0:T(8,128)(2,1)S(1)} %get-tuple-element.40), channel_id=1, source_target_pairs={{0,8},{4,12},{8,0},{12,4},{16,24},{20,28},{24,16},{28,20},{1,9},{5... | collective-permute-start | bytes 122888 | tf_op jit(solution)/shard_map/ppermute | solution.py:19
  207.0 20.9 %collective-permute-start.66 = (bf16[10,2048]{1,0:T(8,128)(2,1)S(1)}, bf16[10,2048]{1,0:T(8,128)(2,1)}, u32[]{:S(2)}, u32[]{:S(2)}) collective-permute-start(bf16[10,2048]{1,0:T(8,128)(2,1)S(1)} %get-tuple-element.39), channel_id=1, source_target_pairs={{0,12},{4,8},{8,4},{12,0},{16,28},{20,24},{24,20},{28,16},{1,13},{... | collective-permute-start | bytes 122888 | tf_op jit(solution)/shard_map/ppermute | solution.py:19
  207.6 21.8 %collective-permute-start.67 = (bf16[10,2048]{1,0:T(8,128)(2,1)}, bf16[10,2048]{1,0:T(8,128)(2,1)}, u32[]{:S(2)}, u32[]{:S(2)}) collective-permute-start(bf16[10,2048]{1,0:T(8,128)(2,1)} %get-tuple-element.38), channel_id=1, source_target_pairs={{0,16},{4,20},{8,24},{12,28},{16,0},{20,4},{24,8},{28,12},{1,17},{... | collective-permute-start | bytes 122888 | tf_op jit(solution)/shard_map/ppermute | solution.py:19
  209.7 22.0 %collective-permute-start.68 = (bf16[10,2048]{1,0:T(8,128)(2,1)}, bf16[10,2048]{1,0:T(8,128)(2,1)}, u32[]{:S(2)}, u32[]{:S(2)}) collective-permute-start(bf16[10,2048]{1,0:T(8,128)(2,1)} %get-tuple-element.37), channel_id=1, source_target_pairs={{0,20},{4,16},{8,28},{12,24},{16,4},{20,0},{24,12},{28,8},{1,21},{... | collective-permute-start | bytes 122888 | tf_op jit(solution)/shard_map/ppermute | solution.py:19
  222.6 14.1 %collective-permute-start.69 = (bf16[10,2048]{1,0:T(8,128)(2,1)}, bf16[10,2048]{1,0:T(8,128)(2,1)S(1)}, u32[]{:S(2)}, u32[]{:S(2)}) collective-permute-start(bf16[10,2048]{1,0:T(8,128)(2,1)} %get-tuple-element.36), channel_id=1, source_target_pairs={{0,24},{4,28},{8,16},{12,20},{16,8},{20,12},{24,0},{28,4},{1,25},{... | collective-permute-start | bytes 122888 | tf_op jit(solution)/shard_map/ppermute | solution.py:19
  227.9 21.9 %collective-permute-start.51 = (bf16[32,2048]{1,0:T(8,128)(2,1)}, bf16[32,2048]{1,0:T(8,128)(2,1)S(1)}, u32[]{:S(2)}, u32[]{:S(2)}) collective-permute-start(bf16[32,2048]{1,0:T(8,128)(2,1)} %get-tuple-element.24), channel_id=1, source_target_pairs={{0,1},{1,0},{2,3},{3,2},{4,5},{5,4},{6,7},{7,6},{8,9},{9,8},{10,11... | collective-permute-start | bytes 393224 | tf_op jit(solution)/shard_map/ppermute | solution.py:19
  229.3 23.9 %collective-permute-start.52 = (bf16[32,2048]{1,0:T(8,128)(2,1)}, bf16[32,2048]{1,0:T(8,128)(2,1)}, u32[]{:S(2)}, u32[]{:S(2)}) collective-permute-start(bf16[32,2048]{1,0:T(8,128)(2,1)} %get-tuple-element.25), channel_id=1, source_target_pairs={{0,2},{1,3},{2,0},{3,1},{4,6},{5,7},{6,4},{7,5},{8,10},{9,11},{10,... | collective-permute-start | bytes 393224 | tf_op jit(solution)/shard_map/ppermute | solution.py:19
  231.7 21.5 %collective-permute-start.53 = (bf16[32,2048]{1,0:T(8,128)(2,1)}, bf16[32,2048]{1,0:T(8,128)(2,1)}, u32[]{:S(2)}, u32[]{:S(2)}) collective-permute-start(bf16[32,2048]{1,0:T(8,128)(2,1)} %get-tuple-element.26), channel_id=1, source_target_pairs={{0,3},{1,2},{2,1},{3,0},{4,7},{5,6},{6,5},{7,4},{8,11},{9,10},{10,... | collective-permute-start | bytes 393224 | tf_op jit(solution)/shard_map/ppermute | solution.py:19
  248.8 14.3 %collective-permute-start.72 = (bf16[32,2048]{1,0:T(8,128)(2,1)S(1)}, bf16[32,2048]{1,0:T(8,128)(2,1)S(1)}, u32[]{:S(2)}, u32[]{:S(2)}) collective-permute-start(bf16[32,2048]{1,0:T(8,128)(2,1)S(1)} %get-tuple-element.22), channel_id=1, source_target_pairs={{0,2},{1,3},{2,0},{3,1},{4,6},{5,7},{6,4},{7,5},{8,10},{9,11},{10,... | collective-permute-start | bytes 393224 | tf_op jit(solution)/shard_map/ppermute | solution.py:19
  249.7 13.5 %collective-permute-start.73 = (bf16[32,2048]{1,0:T(8,128)(2,1)S(1)}, bf16[32,2048]{1,0:T(8,128)(2,1)S(1)}, u32[]{:S(2)}, u32[]{:S(2)}) collective-permute-start(bf16[32,2048]{1,0:T(8,128)(2,1)S(1)} %get-tuple-element.23), channel_id=1, source_target_pairs={{0,3},{1,2},{2,1},{3,0},{4,7},{5,6},{6,5},{7,4},{8,11},{9,10},{10,... | collective-permute-start | bytes 393224 | tf_op jit(solution)/shard_map/ppermute | solution.py:19
  254.3 17.6 %collective-permute-start.54 = (bf16[32,2048]{1,0:T(8,128)(2,1)S(1)}, bf16[32,2048]{1,0:T(8,128)(2,1)S(1)}, u32[]{:S(2)}, u32[]{:S(2)}) collective-permute-start(bf16[32,2048]{1,0:T(8,128)(2,1)S(1)} %fusion.60), channel_id=1, source_target_pairs={{0,1},{1,0},{2,3},{3,2},{4,5},{5,4},{6,7},{7,6},{8,9},{9,8},{10,11... | collective-permute-start | bytes 393224 | tf_op jit(solution)/shard_map/ppermute | solution.py:19
  254.4 20.8 %collective-permute-start.55 = (bf16[32,2048]{1,0:T(8,128)(2,1)S(1)}, bf16[32,2048]{1,0:T(8,128)(2,1)S(1)}, u32[]{:S(2)}, u32[]{:S(2)}) collective-permute-start(bf16[32,2048]{1,0:T(8,128)(2,1)S(1)} %fusion.60), channel_id=1, source_target_pairs={{0,2},{1,3},{2,0},{3,1},{4,6},{5,7},{6,4},{7,5},{8,10},{9,11},{10,... | collective-permute-start | bytes 393224 | tf_op jit(solution)/shard_map/ppermute | solution.py:19
  255.6 19.6 %collective-permute-start.56 = (bf16[32,2048]{1,0:T(8,128)(2,1)S(1)}, bf16[32,2048]{1,0:T(8,128)(2,1)S(1)}, u32[]{:S(2)}, u32[]{:S(2)}) collective-permute-start(bf16[32,2048]{1,0:T(8,128)(2,1)S(1)} %fusion.60), channel_id=1, source_target_pairs={{0,3},{1,2},{2,1},{3,0},{4,7},{5,6},{6,5},{7,4},{8,11},{9,10},{10,... | collective-permute-start | bytes 393224 | tf_op jit(solution)/shard_map/ppermute | solution.py:19
  264.1 14.4 %collective-permute-start.74 = (bf16[32,2048]{1,0:T(8,128)(2,1)S(1)}, bf16[32,2048]{1,0:T(8,128)(2,1)}, u32[]{:S(2)}, u32[]{:S(2)}) collective-permute-start(bf16[32,2048]{1,0:T(8,128)(2,1)S(1)} %fusion.57), channel_id=1, source_target_pairs={{0,1},{1,0},{2,3},{3,2},{4,5},{5,4},{6,7},{7,6},{8,9},{9,8},{10,11... | collective-permute-start | bytes 393224 | tf_op jit(solution)/shard_map/ppermute | solution.py:19
  271.8 12.6 %collective-permute-start.75 = (bf16[32,2048]{1,0:T(8,128)(2,1)S(1)}, bf16[32,2048]{1,0:T(8,128)(2,1)}, u32[]{:S(2)}, u32[]{:S(2)}) collective-permute-start(bf16[32,2048]{1,0:T(8,128)(2,1)S(1)} %fusion.57), channel_id=1, source_target_pairs={{0,2},{1,3},{2,0},{3,1},{4,6},{5,7},{6,4},{7,5},{8,10},{9,11},{10,... | collective-permute-start | bytes 393224 | tf_op jit(solution)/shard_map/ppermute | solution.py:19
  271.8 12.6 %collective-permute-start.76 = (bf16[32,2048]{1,0:T(8,128)(2,1)S(1)}, bf16[32,2048]{1,0:T(8,128)(2,1)}, u32[]{:S(2)}, u32[]{:S(2)}) collective-permute-start(bf16[32,2048]{1,0:T(8,128)(2,1)S(1)} %fusion.57), channel_id=1, source_target_pairs={{0,3},{1,2},{2,1},{3,0},{4,7},{5,6},{6,5},{7,4},{8,11},{9,10},{10,... | collective-permute-start | bytes 393224 | tf_op jit(solution)/shard_map/ppermute | solution.py:19
  (100 other events, 1028.2 us)
